TPU v7x, 32 devices: a whole 2x2x4 slice. The times are simulated.
32 devices in a mesh: prow: 16 (over z, y, core), pcol: 2 (over x).
Axes of the slice: x: 2, y: 2, z: 4, core: 2. Of those that a mesh axis runs over, the one named last changes fastest.
Arguments:
- inverse: float32 [2048, 2048], P('prow', 'pcol'), may hold values from -12 to 12, as said below
- factor_one: bfloat16 [2048, 512], P('prow'), may hold values from -0.1875 to 0.1875
- factor_two: bfloat16 [2048, 512], P('prow'), may hold values from -0.1875 to 0.1875
- factor_top: bfloat16 [512, 512], replicated, may hold values from -0.1875 to 0.1875
- diag_one: float32 [512, 512], replicated, may hold values from -2 to 4, as said below
- diag_two: float32 [512, 512], replicated, may hold values from -2 to 4, as said below
- pattern: int32 [2, 8], replicated, may hold values from 0 to 15, as said below
Outputs:
- inv_cols_one: float32 [2048, 512], P(('prow', 'pcol'))
- diag_block_one: float32 [512, 512], replicated
- inv_cols_two: float32 [2048, 512], P(('prow', 'pcol'))
- inv_top_two: float32 [512, 512], replicated
- diag_block_two: float32 [512, 512], replicated
Inputs may be any that keep to these rules, and one draw needn't show every extreme that they name: `pattern`: each row lists 8 distinct ancestor blocks in rising order; blocks 0 and 8 are in both rows. `inverse`: Symmetric. `diag_one`: Symmetric. `diag_two`: Symmetric.
All inputs are finite; a program needn't handle non-finite values.
Results may differ from a plain program's by a relative error of at most 0.0003.
Values may be sent and summed in bfloat16 or wider, within the bound.
A program may use at most 64 MiB of HBM per device.

v0:
```python
import jax
import jax.numpy as jnp
from jax import lax
from jax.sharding import PartitionSpec as P

BLOCK = 128
highest_precision = lax.Precision.HIGHEST


def broadcast(x, axis, root):
    mine = lax.axis_index(axis) == root
    return lax.psum(jnp.where(mine, x, jnp.zeros_like(x)), axis)


def product(left, right):
    return jnp.dot(left, right, precision=highest_precision, preferred_element_type=jnp.float32)


def row_mask(pattern_row, leading_row_index, row_count):
    row_ids = leading_row_index + lax.iota(jnp.int32, row_count)
    hits = (row_ids // BLOCK)[:, None] == pattern_row[None, :]
    return jnp.max(hits.astype(jnp.float32), axis=1)


def masked(columns, column_mask):
    return columns * column_mask[:, None].astype(jnp.bfloat16)


def multiply(inverse, columns):
    return product(inverse, columns)


def fetch_columns(factor_local, group_ratio, column_group):
    pieces = []
    for offset in range(group_ratio):
        pieces.append(broadcast(factor_local, "prow", group_ratio * column_group + offset))
    return jnp.concatenate(pieces, axis=0)


def reduce_rows(inverse, columns):
    return lax.psum_scatter(multiply(inverse, columns), "pcol", scatter_dimension=0, tiled=True)


def block_sums(inv_cols_one, own_one, own_two):
    correction = product(own_one.T, inv_cols_one)
    mirrored = product(inv_cols_one.T, own_two)
    return lax.psum((correction, mirrored), ("prow", "pcol"))


def shards(inverse, factor_one, factor_two, factor_top, diag_one, diag_two, pattern):
    row_count = inverse.shape[0]
    column_count = inverse.shape[1]
    pcol_size = lax.axis_size("pcol")
    group_ratio = lax.axis_size("prow") // pcol_size
    row_group = lax.axis_index("prow")
    column_group = lax.axis_index("pcol")
    keep_rows = row_count // pcol_size
    row_first = row_group * row_count
    column_first = column_group * column_count
    own_local = column_group * keep_rows
    own_first = row_first + own_local
    own_mask_one = row_mask(pattern[0], own_first, keep_rows)
    own_mask_two = row_mask(pattern[1], own_first, keep_rows)
    own_one = (
        lax.dynamic_slice_in_dim(factor_one, own_local, keep_rows, 0).astype(jnp.float32)
        * own_mask_one[:, None]
    )
    own_two = (
        lax.dynamic_slice_in_dim(factor_two, own_local, keep_rows, 0).astype(jnp.float32)
        * own_mask_two[:, None]
    )
    column_mask_one = row_mask(pattern[0], column_first, column_count)
    column_mask_two = row_mask(pattern[1], column_first, column_count)
    columns_one = masked(fetch_columns(factor_one, group_ratio, column_group), column_mask_one)
    share_one = reduce_rows(inverse, columns_one)
    inv_cols_one = -(own_mask_one[:, None] * share_one)
    correction_one, mirrored = block_sums(inv_cols_one, own_one, own_two)
    columns_two = masked(fetch_columns(factor_two, group_ratio, column_group), column_mask_two)
    share_two = reduce_rows(inverse, columns_two)
    diag_block_one = diag_one - correction_one
    inv_cols_two = -(own_mask_two[:, None] * (share_two + product(inv_cols_one, factor_top)))
    inv_top_two = -(mirrored + product(diag_block_one, factor_top))
    correction_two = lax.psum(product(own_two.T, inv_cols_two), ("prow", "pcol"))
    diag_block_two = diag_two - correction_two - product(factor_top.T, inv_top_two)
    return (inv_cols_one, diag_block_one, inv_cols_two, inv_top_two, diag_block_two)


def solution(mesh):
    in_specs = (P("prow", "pcol"), P("prow", None), P("prow", None), P(), P(), P(), P())
    out_specs = (P(("prow", "pcol"), None), P(), P(("prow", "pcol"), None), P(), P())
    return jax.shard_map(shards, mesh=mesh, in_specs=in_specs, out_specs=out_specs, check_vma=False)
```

profile of v0, /device:TPU:0, one launch (start us, length us, event | category | flops | bytes accessed | tf_op | source)
XLA Modules:
  0.0 309.8 jit_solution(8373516454459245324)
XLA Ops:
  7.2 0.0 all-reduce.7.cloned.1.call-start
  7.2 2.3 broadcast_select_fusion
  9.6 0.0 reduce-scatter.7.cloned.1.call-start
  9.7 0.8 copy-done.10
  10.5 0.1 copy.31
  10.7 0.7 copy-done.26
  11.3 0.1 convert_reduce_fusion.2
  11.4 0.1 convert_reduce_fusion
  11.5 107.1 %all-reduce.7.cloned.1.call-done = (bf16[128,512]{1,0:T(8,128)(2,1)}, bf16[128,512]{1,0:T(8,128)(2,1)}, bf16[128,512]{1,0:T(8,128)(2,1)}, bf16[128,512]{1,0:T(8,...) async-done(((bf16[128,512]{1,0:T(8,128)(2,1)}, ...) | async-done | bytes 2097168 | tf_op jit(solution)/shard_map/psum | solution.py:12
  118.6 0.9 constant_dynamic-update-slice_fusion.7
  119.6 0.9 copy-done.24
  120.5 0.9 copy-done.23
  121.4 0.0 copy-done.22
  121.5 0.8 copy-done.21
  122.3 0.0 copy-done.20
  122.4 0.9 copy-done.19
  123.3 1.4 convolution_bitcast_fusion.2
  124.7 0.8 copy.27
  125.6 0.0 reduce-scatter.7.cloned.1.call-update
  125.6 0.0 reduce-scatter.9.cloned.1.call-start
  125.6 0.8 copy-done.18
  126.5 0.9 copy-done.17
  127.4 0.9 copy-done.16
  128.3 0.9 copy-done.15
  129.2 0.9 copy-done.14
  130.1 0.9 copy-done.13
  131.0 0.9 copy-done.12
  131.9 0.9 copy-done.11
  132.8 1.4 convolution_bitcast_fusion.1
  134.2 0.8 copy.29
  135.0 0.0 reduce-scatter.9.cloned.1.call-update
  135.1 0.0 all-reduce.5.cloned.1.call-start
  135.1 2.1 reduce-scatter.7.cloned.1.call-done
  137.2 1.0 copy.28
  138.3 0.9 copy-done.8
  139.2 2.0 fusion.12
  141.2 2.0 fusion.8
  143.2 8.6 %reduce-scatter.9.cloned.1.call-done = f32[64,512]{1,0:T(8,128)} async-done(((f32[128,512]{1,0:T(8,128)}), f32[64,512]{1,0:T(8,128)}) %reduce-scatter.9.cloned.1.call-update) | async-done | bytes 131088 | tf_op jit(solution)/shard_map/reduce_scatter | solution.py:41
  151.8 1.3 fusion.3
  153.1 2.1 fusion.11
  155.2 0.0 all-reduce.5.cloned.1.call-update
  155.2 0.8 copy.25
  156.0 141.7 %all-reduce.5.cloned.1.call-done = (f32[512,512]{1,0:T(8,128)}, f32[512,512]{1,0:T(8,128)}, f32[512,512]{1,0:T(8,128)}) async-done(((f32[512,512]{1,0:T(8,128)}, f32[512,512]{1,0:T(8,128)}, f32[512,512]{1,0:T(8,128)}), (f32[512,512]{1,0:T(8,128)}, f32[512,512]{1,0:T(8,128)}, f32[512,512]{1,0:T(8,128)})) %all-reduce.5.cloned.1.call-update) | async-done | bytes 3145744 | tf_op jit(solution)/shard_map/psum | solution.py:47
  297.7 1.5 sub.27
  299.2 1.0 fusion
  300.3 0.6 copy-done.6
  300.8 0.3 copy-done.7
  301.1 2.1 fusion.1
  (56 shorter events, 0.3 us)
Async XLA Ops:
  7.2 144.6 %copy-start = (bf16[512,512]{1,0:T(8,128)(2,1)S(1)}, bf16[512,512]{1,0:T(8,128)(2,1)}, u32[]{:S(2)}) copy-start(bf16[512,512]{1,0:T(8,128)(2,1)} %param.10) | copy-start | bytes 1572868
  7.2 111.4 %all-reduce.7.cloned.1.call-start = ((), (), s32[]{:S(2)}) async-start(), calls=%async_computation.5 | async-start | bytes 4194304 | tf_op jit(solution)/shard_map/psum | solution.py:12
  9.6 0.9 copy-start.10
  9.6 127.6 %reduce-scatter.7.cloned.1.call-start = ((), (), s32[]{:S(2)}) async-start(), calls=%async_computation.2 | async-start | bytes 393216
  10.6 0.7 copy-start.26
  118.6 1.0 copy-start.25
  119.6 0.9 copy-start.24
  120.5 0.9 copy-start.23
  120.5 1.0 copy-start.22
  121.4 0.9 copy-start.21
  121.4 1.0 copy-start.20
  121.5 1.8 copy-start.3
  122.4 0.9 copy-start.19
  125.6 0.9 copy-start.18
  125.6 26.2 %reduce-scatter.9.cloned.1.call-start = ((), (), s32[]{:S(2)}) async-start(), calls=%async_computation.3 | async-start | bytes 393216 | tf_op jit(solution)/shard_map/reduce_scatter | solution.py:41
  126.5 0.9 copy-start.17
  127.4 0.9 copy-start.16
  128.3 0.9 copy-start.15
  129.2 0.9 copy-start.14
  130.1 0.9 copy-start.13
  131.0 0.9 copy-start.12
  131.9 0.9 copy-start.11
  135.1 162.6 %all-reduce.5.cloned.1.call-start = ((), (), s32[]{:S(2)}) async-start(), calls=%async_computation.4 | async-start | bytes 6291456 | tf_op jit(solution)/shard_map/psum | solution.py:47
  138.3 0.9 copy-start.8
  153.1 2.1 copy-start.9
  155.2 142.5 %copy-start.4 = (f32[512,512]{1,0:T(8,128)S(1)}, f32[512,512]{1,0:T(8,128)}, u32[]{:S(2)}) copy-start(f32[512,512]{1,0:T(8,128)} %param.11) | copy-start | bytes 3145732
  297.7 1.5 copy-start.5
  299.2 1.0 copy-start.1
  299.2 1.6 copy-start.6
  299.2 1.9 copy-start.7
  300.3 3.0 copy-start.2
Sparse Core Ops, SparseCore 0:
  14.0 104.6 all-reduce.6
  125.7 11.4 reduce-scatter.6
  140.0 11.6 reduce-scatter.8
  159.0 138.6 all-reduce.4
where the time goes:
time: 310 us
  waiting for transfers between devices  260 us (84%)
  local copies, waits for them, and re-layouts  18.6 us (6%)
  between operations  14 us (5%)
  matrix products  13.3 us (4%)
  other arithmetic  4.09 us (1%)
    psum x1, waiting for transfers between devices, block_sums(): return lax.psum((correction, mirrored), ('prow', 'pcol'))  142 us
    psum x1, waiting for transfers between devices, broadcast(): return lax.psum(jnp.where(mine, x, jnp.zeros_like(x)), axis)  107 us
    unnamed x73, local copies, waits for them, and re-layouts  18.6 us
    dot_general x8, matrix products, product(): jnp.dot(left, right, precision=highest_precision, preferred_element_type=...  13.3 us
    reduce_scatter x1, waiting for transfers between devices, reduce_rows(): lax.psum_scatter(multiply(inverse, columns), 'pcol', scatter_dimension=0,...  8.6 us
  transfers between devices with their start and end apart: 4, of which 4 were waited for; matrix products, arithmetic and copies ran while one was open for 3% of the time, Pallas kernels for 0%

commit v1 on v0

--- a/solution.py
+++ b/solution.py
@@ -44,7 +44,7 @@
 def block_sums(inv_cols_one, own_one, own_two):
     correction = product(own_one.T, inv_cols_one)
     mirrored = product(inv_cols_one.T, own_two)
-    return lax.psum((correction, mirrored), ("prow", "pcol"))
+    return lax.psum(lax.psum((correction, mirrored), "pcol"), "prow")
 
 
 def shards(inverse, factor_one, factor_two, factor_top, diag_one, diag_two, pattern):

time: 310 us -> 468 us (1.51)
  waiting for transfers between devices: 260 us -> 417 us
    psum x1 -> x3, waiting for transfers between devices: 142 us -> 284 us  [the longest x2 151 us: block_sums(): return lax.psum(lax.psum((correction, mirrored), 'pcol'), 'prow')]
    unnamed x5 -> x7, waiting for transfers between devices: 2.18 us -> 10.6 us
    reduce_scatter x1, waiting for transfers between devices: 8.6 us -> 14.4 us  [reduce_rows(): lax.psum_scatter(multiply(inverse, columns), 'pcol', scatter_dimension=0,...]
    unnamed x73 -> x69, local copies, waits for them, and re-layouts: 18.6 us -> 16.9 us
  transfers between devices with their start and end apart: 4 -> 6, of which waited for: 4 -> 6; matrix products, arithmetic and copies ran while one was open for 3% -> 2% of each run, Pallas kernels for 0% -> 0%
where the time goes in v1:
time: 468 us
  waiting for transfers between devices  417 us (89%)
  local copies, waits for them, and re-layouts  17 us (4%)
  matrix products  14.7 us (3%)
  between operations  14.4 us (3%)
    psum x2, waiting for transfers between devices, block_sums(): return lax.psum(lax.psum((correction, mirrored), 'pcol'), 'prow')  151 us
    psum x1, waiting for transfers between devices, shards(): lax.psum(product(own_two.T, inv_cols_two), ('prow', 'pcol'))  133 us
    psum x1, waiting for transfers between devices, broadcast(): return lax.psum(jnp.where(mine, x, jnp.zeros_like(x)), axis)  108 us
    unnamed x69, local copies, waits for them, and re-layouts  16.9 us
    dot_general x8, matrix products, product(): jnp.dot(left, right, precision=highest_precision, preferred_element_type=...  14.7 us
    reduce_scatter x1, waiting for transfers between devices, reduce_rows(): lax.psum_scatter(multiply(inverse, columns), 'pcol', scatter_dimension=0,...  14.4 us
    unnamed x7, waiting for transfers between devices  10.6 us
  transfers between devices with their start and end apart: 6, of which 6 were waited for; matrix products, arithmetic and copies ran while one was open for 2% of the time, Pallas kernels for 0%

profile of v1, /device:TPU:0, one launch (start us, length us, event | category | flops | bytes accessed | tf_op | source)
XLA Modules:
  0.0 467.7 jit_solution(4237819168914070375)
XLA Ops:
  7.2 0.0 all-reduce.14.cloned.1.call-start
  7.2 2.3 broadcast_select_fusion
  9.6 0.0 all-reduce.14.cloned.1.call-update
  9.6 0.0 reduce-scatter.7.cloned.1.call-start
  9.7 0.7 copy-done.24
  10.3 0.1 convert_reduce_fusion
  10.4 108.2 %all-reduce.14.cloned.1.call-done = (bf16[128,512]{1,0:T(8,128)(2,1)}, bf16[128,512]{1,0:T(8,128)(2,1)}, bf16[128,512]{1,0:T(8,128)(2,1)}, bf16[128,512]{1,0:T(8...) async-done(((bf16[128,512]{1,0:T(8,128)(2,1)}, ...) | async-done | bytes 2097168 | tf_op jit(solution)/shard_map/psum | solution.py:12
  118.6 0.9 constant_dynamic-update-slice_fusion.7
  119.6 0.9 copy-done.22
  120.5 0.9 copy-done.21
  121.4 0.0 copy-done.20
  121.5 0.8 copy-done.19
  122.3 0.0 copy-done.18
  122.4 0.9 copy-done.17
  123.3 1.4 convolution_bitcast_fusion.2
  124.7 0.8 copy.27
  125.6 0.0 all-reduce.12.cloned.1.call-start
  125.6 0.8 copy-done.8
  126.5 0.1 copy.31
  126.6 0.1 convert_reduce_fusion.2
  126.7 10.5 %reduce-scatter.7.cloned.1.call-done = f32[64,512]{1,0:T(8,128)} async-done(((f32[128,512]{1,0:T(8,128)}), f32[64,512]{1,0:T(8,128)}) %reduce-scatter.7.cloned.1.call-update) | async-done | bytes 131088
  137.2 1.0 copy.28
  138.3 2.0 fusion.8
  140.3 2.0 fusion.12
  142.3 0.0 reduce-scatter.9.cloned.1.call-start
  142.4 0.8 copy-done.16
  143.2 0.9 copy-done.15
  144.1 0.9 copy-done.14
  145.0 0.9 copy-done.13
  145.9 0.9 copy-done.12
  146.8 0.9 copy-done.11
  147.8 0.9 copy-done.10
  148.7 0.9 copy-done.9
  149.6 1.4 convolution_bitcast_fusion.1
  151.0 0.8 copy.29
  151.9 0.0 all-reduce.10.cloned.1.call-start
  151.9 53.7 %all-reduce.12.cloned.1.call-done = (f32[512,512]{1,0:T(8,128)}, f32[512,512]{1,0:T(8,128)}) async-done(((f32[512,512]{1,0:T(8,128)}, f32[512,512]{1,0:T(8,128)}), (f32[512,512]{1,0:T(8,128)}, f32[512,512]{1,0:T(8,128)})) %all-reduce.12.cloned.1.call-update) | async-done | bytes 2097168 | tf_op jit(solution)/shard_map/psum | solution.py:47
  205.6 0.0 all-reduce.8.cloned.1.call-start
  205.7 14.4 %reduce-scatter.9.cloned.1.call-done = f32[64,512]{1,0:T(8,128)} async-done(((f32[128,512]{1,0:T(8,128)}), f32[64,512]{1,0:T(8,128)}) %reduce-scatter.9.cloned.1.call-update) | async-done | bytes 131088 | tf_op jit(solution)/shard_map/reduce_scatter | solution.py:41
  220.0 1.3 fusion.3
  221.4 2.1 fusion.11
  223.4 0.0 all-reduce.8.cloned.1.call-update
  223.5 0.8 copy.25
  224.2 97.2 %all-reduce.10.cloned.1.call-done = (f32[512,512]{1,0:T(8,128)}, f32[512,512]{1,0:T(8,128)}) async-done(((f32[512,512]{1,0:T(8,128)}, f32[512,512]{1,0:T(8,128)}), (f32[512,512]{1,0:T(8,128)}, f32[512,512]{1,0:T(8,128)})) %all-reduce.10.cloned.1.call-update) | async-done | bytes 2097168 | tf_op jit(solution)/shard_map/psum | solution.py:47
  321.5 1.5 sub.27
  323.0 1.0 fusion
  324.1 133.2 %all-reduce.8.cloned.1.call-done = f32[512,512]{1,0:T(8,128)} async-done(((f32[512,512]{1,0:T(8,128)}), f32[512,512]{1,0:T(8,128)}) %all-reduce.8.cloned.1.call-update) | async-done | bytes 1048592 | tf_op jit(solution)/shard_map/psum | solution.py:83
  457.2 3.6 fusion.1
  (58 shorter events, 0.4 us)
Async XLA Ops:
  7.2 212.9 %copy-start = (bf16[512,512]{1,0:T(8,128)(2,1)S(1)}, bf16[512,512]{1,0:T(8,128)(2,1)}, u32[]{:S(2)}) copy-start(bf16[512,512]{1,0:T(8,128)(2,1)} %param.10) | copy-start | bytes 1572868
  7.2 111.4 %all-reduce.14.cloned.1.call-start = ((), (), s32[]{:S(2)}) async-start(), calls=%async_computation.7 | async-start | bytes 4194304 | tf_op jit(solution)/shard_map/psum | solution.py:12
  9.6 127.6 %reduce-scatter.7.cloned.1.call-start = ((), (), s32[]{:S(2)}) async-start(), calls=%async_computation.3 | async-start | bytes 393216
  9.7 0.7 copy-start.24
  118.6 1.0 copy-start.23
  119.6 0.9 copy-start.22
  120.5 0.9 copy-start.21
  120.5 1.0 copy-start.20
  121.4 0.9 copy-start.19
  121.4 1.0 copy-start.18
  121.5 1.8 copy-start.3
  122.4 0.9 copy-start.17
  125.6 0.9 copy-start.8
  125.6 80.0 %all-reduce.12.cloned.1.call-start = ((), (), s32[]{:S(2)}) async-start(), calls=%async_computation.6 | async-start | bytes 4194304 | tf_op jit(solution)/shard_map/psum | solution.py:47
  138.3 2.0 copy-start.6
  142.3 0.9 copy-start.16
  142.3 77.7 %reduce-scatter.9.cloned.1.call-start = ((), (), s32[]{:S(2)}) async-start(), calls=%async_computation.4 | async-start | bytes 393216 | tf_op jit(solution)/shard_map/reduce_scatter | solution.py:41
  143.2 0.9 copy-start.15
  144.1 0.9 copy-start.14
  145.0 0.9 copy-start.13
  145.9 0.9 copy-start.12
  146.8 0.9 copy-start.11
  147.7 0.9 copy-start.10
  148.7 0.9 copy-start.9
  151.9 169.6 %all-reduce.10.cloned.1.call-start = ((), (), s32[]{:S(2)}) async-start(), calls=%async_computation.5 | async-start | bytes 4194304 | tf_op jit(solution)/shard_map/psum | solution.py:47
  205.6 251.6 %all-reduce.8.cloned.1.call-start = ((), (), s32[]{:S(2)}) async-start(), calls=%async_computation.2 | async-start | bytes 2097152 | tf_op jit(solution)/shard_map/psum | solution.py:83
  221.3 2.1 copy-start.7
  221.4 100.1 %copy-start.4 = (f32[512,512]{1,0:T(8,128)S(1)}, f32[512,512]{1,0:T(8,128)}, u32[]{:S(2)}) copy-start(f32[512,512]{1,0:T(8,128)} %param.11) | copy-start | bytes 3145732
  321.5 1.5 copy-start.5
  323.0 1.0 copy-start.1
  324.1 136.8 %copy-start.2 = (f32[512,512]{1,0:T(8,128)}, f32[512,512]{1,0:T(8,128)S(1)}, u32[]{:S(2)}) copy-start(f32[512,512]{1,0:T(8,128)S(1)} %fusion) | copy-start | bytes 3145732
Sparse Core Ops, SparseCore 0:
  14.0 104.6 all-reduce.13
  125.7 11.4 reduce-scatter.6
  142.4 63.1 all-reduce.11
  208.3 11.6 reduce-scatter.8
  223.5 97.9 all-reduce.9
  327.9 129.2 all-reduce.7
